TPU v7x, 32 devices: a whole 2x2x4 slice. The times are simulated.
32 devices in a mesh: groups: 2 (over y), ctx: 16 (over z, x, core).
Axes of the slice: x: 2, y: 2, z: 4, core: 2. Of those that a mesh axis runs over, the one named last changes fastest.
Arguments:
- child_q: bfloat16 [32, 128, 4096], P(('groups', 'ctx')), parts along dimension 0, may hold values from -8 to 8
- child_kv: bfloat16 [32, 128, 2, 512], P(('groups', 'ctx')), parts along dimension 0, may hold values from -12 to 12
- prompt_kv: bfloat16 [128, 2, 512], P(('groups', 'ctx')), parts along dimension 0, may hold values from -12 to 12
- parent_kv: bfloat16 [256, 2, 2, 512], P(('groups', 'ctx')), parts along dimension 0, may hold values from -12 to 12
- fork_list: int32 [32], P('groups'), parts along dimension 0, may hold values from 0 to 1
- owner_map: int32 [4, 16], P('groups'), parts along dimension 0, may hold values from 0 to 15, each once within a row
- lengths: int32 [4], P('groups'), parts along dimension 0, may hold values from 1 to 128, as said below
Outputs:
- child_out: bfloat16 [32, 128, 4096], P(('groups', 'ctx')), parts along dimension 0
There are 2 independent parts, one for each index of `groups`. A program takes and returns all parts, laid end to end along the dimension named above; each array names one. Nothing has to cross between parts.
Inputs may be any that keep to these rules, and one draw needn't show every extreme that they name: `lengths`: some parent has all 128 positions valid.
All inputs are finite; a program needn't handle non-finite values.
Results may differ from a plain program's by a relative error of at most 0.0032.
Values may be sent and summed in bfloat16 or wider, within the bound.
A program may use at most 64 MiB of HBM per device.

v0:
```python
import jax
import jax.numpy as jnp
from jax import lax
from jax.sharding import PartitionSpec as P

KVH = 4
HD = 128


def head_rows(queries, kv_head, group_size, head_dim):
    row_count = queries.shape[0]
    column_block = queries[
        :, kv_head * group_size * head_dim : (kv_head + 1) * group_size * head_dim
    ]
    return column_block.reshape(row_count * group_size, head_dim)


def level_part(queries, key_rows, value_rows, allowed):
    scaling = queries.shape[1] ** (-0.5)
    scores = (
        jnp.einsum("qd,kd->qk", queries, key_rows, preferred_element_type=jnp.float32) * scaling
    )
    if allowed is not None:
        scores = jnp.where(allowed, scores, -jnp.inf)
    highest = jnp.max(scores, axis=1)
    weights = jnp.exp(scores - highest[:, None])
    if allowed is not None:
        weights = jnp.where(allowed, weights, 0.0)
    weights = lax.optimization_barrier(weights.astype(jnp.bfloat16))
    totals = jnp.sum(weights.astype(jnp.float32), axis=1)
    weighted = jnp.dot(weights, value_rows, preferred_element_type=jnp.float32)
    return (highest, totals, weighted)


def merge_levels(former, latter):
    highest = jnp.maximum(former[0], latter[0])
    weight_one = jnp.exp(former[0] - highest)
    weight_two = jnp.exp(latter[0] - highest)
    totals = former[1] * weight_one + latter[1] * weight_two
    weighted = former[2] * weight_one[:, None] + latter[2] * weight_two[:, None]
    return (highest, totals, weighted)


def body(child_q, child_kv, prompt_kv, parent_kv, fork_list, owner_map, lengths):
    queries = child_q[0]
    own_rows = child_kv[0]
    span_rows = queries.shape[0]
    kv_width = own_rows.shape[2]
    head_dim = HD
    kv_heads = KVH
    group_size = queries.shape[1] // kv_width
    query_rows = span_rows * group_size
    device = lax.axis_index("ctx")
    axis_size = lax.axis_size("ctx")
    seg_rows = parent_kv.shape[0]
    parent = lax.dynamic_index_in_dim(fork_list, device, 0, keepdims=False)
    owner_row = lax.dynamic_index_in_dim(owner_map, parent, 0, keepdims=False)
    places = jnp.arange(axis_size, dtype=jnp.int32)
    matches = owner_row[None, :] == places[:, None]
    pieces = jnp.sum(jnp.where(matches, places[None, :], 0), axis=1)
    positions = jnp.arange(seg_rows, dtype=jnp.int32)[:, None] + pieces[None, :] * seg_rows
    live_length = lax.dynamic_index_in_dim(lengths, parent, 0, keepdims=False)
    allowed = (positions < live_length).reshape(1, seg_rows * axis_size)
    outgoing = jnp.take(parent_kv, fork_list, axis=1)
    query_time = jnp.arange(query_rows, dtype=jnp.int32) // group_size
    causal = jnp.arange(span_rows, dtype=jnp.int32)[None, :] <= query_time[:, None]
    head_queries = []
    for kv_head in range(kv_heads):
        head_queries.append(head_rows(queries, kv_head, group_size, head_dim))
    prompt_copies = jnp.broadcast_to(
        prompt_kv[:, None], (prompt_kv.shape[0], axis_size, 2, kv_width)
    )
    prompt_in, arrived = (
        lax.all_to_all(prompt_copies, "ctx", split_axis=1, concat_axis=1, tiled=True),
        lax.all_to_all(outgoing, "ctx", split_axis=1, concat_axis=1, tiled=True),
    )
    prompt_all = prompt_in.reshape(prompt_kv.shape[0] * axis_size, 2, kv_width)
    segment = arrived.reshape(seg_rows * axis_size, 2, kv_width)
    results = []
    for kv_head in range(kv_heads):
        low = kv_head * head_dim
        prompt_stats = level_part(
            head_queries[kv_head],
            prompt_all[:, 0, low : low + head_dim],
            prompt_all[:, 1, low : low + head_dim],
            None,
        )
        parent_stats = level_part(
            head_queries[kv_head],
            segment[:, 0, low : low + head_dim],
            segment[:, 1, low : low + head_dim],
            allowed,
        )
        own_stats = level_part(
            head_queries[kv_head],
            own_rows[:, 0, low : low + head_dim],
            own_rows[:, 1, low : low + head_dim],
            causal,
        )
        merged = merge_levels(merge_levels(prompt_stats, parent_stats), own_stats)
        results.append((merged[2] / merged[1][:, None]).reshape(span_rows, group_size * head_dim))
    return jnp.concatenate(results, axis=1).astype(jnp.bfloat16)[None]


def solution(mesh):
    placed = (
        P(("groups", "ctx"), None, None),
        P(("groups", "ctx"), None, None, None),
        P(("groups", "ctx"), None, None),
        P(("groups", "ctx"), None, None, None),
        P("groups"),
        P("groups", None),
        P("groups"),
    )
    return jax.shard_map(
        body,
        mesh=mesh,
        in_specs=placed,
        out_specs=P(("groups", "ctx"), None, None),
        check_vma=False,
    )
```

profile of v0, /device:TPU:0, one launch (start us, length us, event | category | flops | bytes accessed | tf_op | source)
XLA Modules:
  0.0 47.7 jit_solution(876810784480943631)
XLA Ops:
  0.0 0.0 copy-start
  0.0 0.7 %copy.17 = bf16[4,2,512]{2,0,1:T(4,128)(2,1)S(1)} copy(bf16[4,2,512]{2,1,0:T(2,128)(2,1)} %param.9) | data formatting | bytes 16384 | tf_op args[2]
  0.7 0.7 %broadcast_in_dim.125 = bf16[4,16,2,512]{3,0,2,1:T(4,128)(2,1)} broadcast(bf16[4,2,512]{2,0,1:T(4,128)(2,1)S(1)} %copy.17), dimensions={0,2,3} | broadcast | bytes 139264 | tf_op jit(solution)/shard_map/broadcast_in_dim | solution.py:70
  1.4 7.4 %all-to-all-start = ((bf16[4,16,2,512]{3,0,2,1:T(4,128)(2,1)}), bf16[4,16,2,512]{3,0,2,1:T(4,128)(2,1)S(1)}, u32[]{:S(2)}, u32[]{:S(2)}) async-start(bf16[4,16,2,512]{3,0,2,1:T(4,128)(2,1)} %broadcast_in_dim.125), calls=%async_computation | async-start | bytes 262144 | tf_op jit(solution)/shard_map/all_to_all | solution.py:74
  8.8 0.7 %compare_select_fusion = s32[16]{0:T(128)S(1)} fusion(s32[16]{0:T(128)} %param.11), kind=kLoop, calls=%fused_computation.149 | loop fusion | flops 48 | bytes 128 | tf_op jit(solution)/shard_map/jit(_take)/jit(_where)/select_n | solution.py:64
  9.4 0.7 %compare_and_fusion = pred[16]{0:T(512)(128)(4,1)S(1)} fusion(s32[16]{0:T(128)} %param.11), kind=kLoop, calls=%fused_computation.150 | loop fusion | flops 96 | bytes 80 | tf_op jit(solution)/shard_map/jit(_take)/and | solution.py:64
  10.1 1.3 %fusion.52 = (bf16[128,1024]{1,0:T(8,128)(2,1)S(1)}, bf16[128,1024]{1,0:T(8,128)(2,1)S(1)}, bf16[128,1024]{1,0:T(8,128)(2,1)S(1)}, bf16[128,1024]{1,0:T(8,128)(2,1)S(1)}) fusion(bf16[128,4096]{1,0:T(8,128)(2,1)} %bitcast.148), kind=kLoop, calls=%fused_computation.153 | loop fusion | bytes 2097152 | tf_op jit(solution)/shard_map/slice | solution.py:12
  11.4 0.1 reshape.330
  11.5 0.0 copy-done.3
  11.6 0.1 reshape.335
  11.7 0.2 fusion.53
  12.0 1.0 %fusion.54 = (f32[1024]{0:T(1024)S(1)}, f32[1024,128]{0,1:T(8,128)}) fusion(bf16[1024,128]{1,0:T(8,128)(2,1)S(1)} %reshape.335, bf16[128,2,512]{2,0,1:T(8,128)(2,1)S(1)} %bitcast.150, s32[1024]{0:T(1024)S(1)} %add_select_fusion), kind=kOutput, calls=%fused_computation.155 | convolution fusion | flops 34077696 | bytes 827392 | tf_op jit(solution)/shard_map/qd,kd->qk/dot_general | solution.py:21
  13.0 0.1 reshape.334
  13.1 0.0 copy-start.5
  13.1 0.0 copy-start.6
  13.1 0.0 copy-start.4
  13.1 1.0 %fusion.55 = (f32[1024]{0:T(1024)S(1)}, f32[1024,128]{0,1:T(8,128)}) fusion(bf16[1024,128]{1,0:T(8,128)(2,1)S(1)} %reshape.334, bf16[128,2,512]{2,0,1:T(8,128)(2,1)S(1)} %bitcast.151, s32[1024]{0:T(1024)S(1)} %add_select_fusion), kind=kOutput, calls=%fused_computation.156 | convolution fusion | flops 34077696 | bytes 827392 | tf_op jit(solution)/shard_map/qd,kd->qk/dot_general | solution.py:21
  14.2 0.1 reshape.333
  14.3 1.0 %fusion.56 = (f32[1024]{0:T(1024)S(1)}, f32[1024,128]{0,1:T(8,128)}) fusion(bf16[1024,128]{1,0:T(8,128)(2,1)S(1)} %reshape.333, bf16[128,2,512]{2,0,1:T(8,128)(2,1)S(1)} %bitcast.152, s32[1024]{0:T(1024)S(1)} %add_select_fusion), kind=kOutput, calls=%fused_computation.157 | convolution fusion | flops 34077696 | bytes 827392 | tf_op jit(solution)/shard_map/qd,kd->qk/dot_general | solution.py:21
  15.3 0.6 %dynamic_slice.12 = s32[1]{0:T(128)} dynamic-slice(s32[16]{0:T(128)S(1)} %copy-done.5, s32[]{:T(128)S(6)} %select_n.100), dynamic_slice_sizes={1} | dynamic-slice | bytes 12 | tf_op jit(solution)/shard_map/jit(dynamic_index_in_dim)/dynamic_slice | solution.py:56
  17.9 0.6 %dynamic_slice.14 = s32[1]{0:T(128)} dynamic-slice(s32[2]{0:T(128)S(1)} %copy-done.6, s32[]{:T(128)S(6)} %select_n.101), dynamic_slice_sizes={1} | dynamic-slice | bytes 12 | tf_op jit(solution)/shard_map/jit(dynamic_index_in_dim)/dynamic_slice | solution.py:62
  18.5 0.1 select_reduce_fusion
  18.6 0.6 %add_compare_fusion = pred[8,16]{1,0:T(8,128)(4,1)S(1)} fusion(s32[]{:T(128)} %bitcast.6, s32[16]{0:T(128)S(1)} %broadcast_multiply_fusion), kind=kLoop, calls=%fused_computation.147 | loop fusion | flops 256 | bytes 196 | tf_op jit(solution)/shard_map/lt | solution.py:63
  19.3 1.7 %select_convert_fusion.7 = (bf16[1024,128]{0,1:T(8,128)(2,1)S(1)}, bf16[1024,128]{0,1:T(8,128)(2,1)S(1)}, bf16[1024,128]{0,1:T(8,128)(2,1)S(1)}, bf16[1024,128]{0,1:T(8,128)(2,1)S(1)}) fusion(f32[1024,128]{0,1:T(8,128)S(1)} %get-tuple-element.38, f32[1024]{0:T(1024)S(1)} %get-tuple-element.37, s32[1024]{0:T(1024)S(1)} %add_select_fusion, ...), kind=kLoop, calls=%fused_computation.69 | loop fusion | flops 1703936 | bytes 3166208 | tf_op jit(solution)/shard_map/convert_element_type | solution.py:29
  21.0 0.1 lt.31
  21.1 0.0 copy-done
  21.1 1.1 %gather_fusion = bf16[16,8,2,512]{3,2,1,0:T(2,128)(2,1)S(1)} fusion(bf16[8,2,2,512]{3,2,1,0:T(2,128)(2,1)S(1)} %copy-done, s32[1024]{0:T(1024)S(1)} %pad_clamp_fusion), kind=kCustom, calls=%fused_computation | custom fusion | bytes 524352 | tf_op jit(solution)/shard_map/jit(_take)/gather | solution.py:64
  22.2 1.0 %fusion.32 = bf16[8,16,2,512]{3,2,0,1:T(2,128)(2,1)} fusion(bf16[16,8,2,512]{3,2,1,0:T(2,128)(2,1)S(1)} %gather_fusion, pred[16]{0:T(512)(128)(4,1)S(1)} %compare_and_fusion), kind=kLoop, calls=%fused_computation.85 | loop fusion | flops 131072 | bytes 524304 | tf_op jit(solution)/shard_map/jit(_take)/select_n | solution.py:64
  23.2 0.0 all-to-all-done
  23.2 6.0 %all-to-all-start.1 = ((bf16[8,16,2,512]{3,2,0,1:T(2,128)(2,1)}), bf16[8,16,2,512]{3,2,0,1:T(2,128)(2,1)S(1)}, u32[]{:S(2)}, u32[]{:S(2)}) async-start(bf16[8,16,2,512]{3,2,0,1:T(2,128)(2,1)} %fusion.32), calls=%async_computation.1 | async-start | bytes 524288 | tf_op jit(solution)/shard_map/all_to_all | solution.py:75
  29.3 0.2 fusion.61
  29.5 0.2 fusion.62
  29.8 0.2 fusion.63
  30.0 0.2 fusion.64
  30.6 8.7 %all-to-all-done.1 = bf16[8,16,2,512]{3,2,0,1:T(2,128)(2,1)S(1)} async-done(((bf16[8,16,2,512]{3,2,0,1:T(2,128)(2,1)}), bf16[8,16,2,512]{3,2,0,1:T(2,128)(2,1)S(1)}, u32[]{:S(2)}, u32[]{:S(2)}) %all-to-all-start.1) | async-done | bytes 262176 | tf_op jit(solution)/shard_map/all_to_all | solution.py:75
  39.3 0.1 copy.19
  39.4 0.2 fusion.57
  39.7 0.2 fusion.58
  39.9 0.2 fusion.59
  40.2 0.2 fusion.60
  40.4 0.4 fusion.28
  40.8 0.0 copy-start.2
  40.9 0.1 convert_reduce_fusion
  41.0 0.3 convolution_multiply_fusion
  41.3 0.3 convolution_multiply_fusion.2
  41.6 0.2 copy-done.2
  41.8 0.6 %fusion.24 = bf16[1024,128]{1,0:T(8,128)(2,1)S(1)} fusion(f32[1024,128]{1,0:T(8,128)S(1)} %convolution_multiply_fusion, f32[1024,128]{1,0:T(8,128)S(1)} %convolution_multiply_fusion.2, bf16[1024,64]{0,1:T(8,128)(2,1)S(1)} %exponential_convert_fusion, f32[1024]{0:T(1024)S(1)} %get-tuple-element.20, f32[1024]{0:T(1024)S(1)} %get-tuple-element.22, ...), kind=kOutput, calls=%fused_computation.45 | convolution fusion | flops 17563648 | bytes 1470464 | tf_op jit(solution)/shard_map/dot_general | solution.py:31
  42.3 0.1 concatenate.22
  42.4 0.1 convert_reduce_fusion.2
  42.6 0.3 convolution_multiply_fusion.5
  42.9 0.3 convolution_multiply_fusion.7
  43.2 0.6 %fusion.25 = bf16[1024,128]{1,0:T(8,128)(2,1)S(1)} fusion(f32[1024,128]{1,0:T(8,128)S(1)} %convolution_multiply_fusion.5, f32[1024,128]{1,0:T(8,128)S(1)} %convolution_multiply_fusion.7, bf16[1024,64]{0,1:T(8,128)(2,1)S(1)} %exponential_convert_fusion.1, f32[1024]{0:T(1024)S(1)} %get-tuple-element.15, f32[1024]{0:T(1024)S(1)} %get-tuple-element.17, ...), kind=kOutput, calls=%fused_computation.46 | convolution fusion | flops 17563648 | bytes 1470464 | tf_op jit(solution)/shard_map/dot_general | solution.py:31
  43.7 0.1 concatenate.21
  43.9 0.1 convert_reduce_fusion.4
  44.0 0.3 convolution_multiply_fusion.10
  44.3 0.3 convolution_multiply_fusion.12
  44.6 0.6 %fusion.26 = bf16[1024,128]{1,0:T(8,128)(2,1)S(1)} fusion(f32[1024,128]{1,0:T(8,128)S(1)} %convolution_multiply_fusion.10, f32[1024,128]{1,0:T(8,128)S(1)} %convolution_multiply_fusion.12, bf16[1024,64]{0,1:T(8,128)(2,1)S(1)} %exponential_convert_fusion.2, f32[1024]{0:T(1024)S(1)} %get-tuple-element.10, f32[1024]{0:T(1024)S(1)} %get-tuple-element.12, ...), kind=kOutput, calls=%fused_computation.47 | convolution fusion | flops 17563648 | bytes 1470464 | tf_op jit(solution)/shard_map/dot_general | solution.py:31
  45.1 0.1 concatenate.20
  45.3 0.1 convert_reduce_fusion.6
  45.4 0.3 convolution_multiply_fusion.15
  45.7 0.3 convolution_multiply_fusion.17
  46.0 0.6 %fusion.27 = bf16[1024,128]{1,0:T(8,128)(2,1)S(1)} fusion(f32[1024,128]{1,0:T(8,128)S(1)} %convolution_multiply_fusion.15, f32[1024,128]{1,0:T(8,128)S(1)} %convolution_multiply_fusion.17, bf16[1024,64]{0,1:T(8,128)(2,1)S(1)} %exponential_convert_fusion.3, f32[1024]{0:T(1024)S(1)} %get-tuple-element.5, f32[1024]{0:T(1024)S(1)} %get-tuple-element.7, ...), kind=kOutput, calls=%fused_computation.48 | convolution fusion | flops 17563648 | bytes 1470464 | tf_op jit(solution)/shard_map/dot_general | solution.py:31
  46.6 0.1 concatenate.19
  46.7 1.0 %pad_maximum_fusion = bf16[1,128,4096]{2,1,0:T(8,128)(2,1)} fusion(bf16[1,128,1024]{2,1,0:T(8,128)(2,1)S(1)} %concatenate.22, bf16[1,128,1024]{2,1,0:T(8,128)(2,1)S(1)} %concatenate.21, bf16[1,128,1024]{2,1,0:T(8,128)(2,1)S(1)} %concatenate.20, bf16[1,128,1024]{2,1,0:T(8,128)(2,1)S(1)} %concatenate.19), kind=kLoop, calls=%fused_computation.53 | loop fusion | flops 4194304 | bytes 2097152 | tf_op jit(solution)/shard_map/concatenate | solution.py:102
  (24 shorter events, 0.5 us)
Async XLA Ops:
  0.0 21.1 %copy-start = (bf16[8,2,2,512]{3,2,1,0:T(2,128)(2,1)S(1)}, bf16[8,2,2,512]{3,2,1,0:T(2,128)(2,1)}, u32[]{:S(2)}) copy-start(bf16[8,2,2,512]{3,2,1,0:T(2,128)(2,1)} %param.10) | copy-start | bytes 98308
  1.4 21.8 %all-to-all-start = ((bf16[4,16,2,512]{3,0,2,1:T(4,128)(2,1)}), bf16[4,16,2,512]{3,0,2,1:T(4,128)(2,1)S(1)}, u32[]{:S(2)}, u32[]{:S(2)}) async-start(bf16[4,16,2,512]{3,0,2,1:T(4,128)(2,1)} %broadcast_in_dim.125), calls=%async_computation | async-start | bytes 262144 | tf_op jit(solution)/shard_map/all_to_all | solution.py:74
  10.1 1.4 %copy-start.3 = (bf16[1,128,2,512]{3,2,1,0:T(2,128)(2,1)S(1)}, bf16[1,128,2,512]{3,2,1,0:T(2,128)(2,1)}, u32[]{:S(2)}) copy-start(bf16[1,128,2,512]{3,2,1,0:T(2,128)(2,1)} %param.8) | copy-start | bytes 786436
  13.1 2.2 %copy-start.5 = (s32[16]{0:T(128)S(1)}, s32[16]{0:T(128)}, u32[]{:S(2)}) copy-start(s32[16]{0:T(128)} %param.11) | copy-start | bytes 196
  13.1 4.7 %copy-start.6 = (s32[2]{0:T(128)S(1)}, s32[2]{0:T(128)}, u32[]{:S(2)}) copy-start(s32[2]{0:T(128)} %param.13) | copy-start | bytes 28
  13.1 5.4 %copy-start.4 = (s32[2,16]{1,0:T(2,128)S(1)}, s32[2,16]{1,0:T(2,128)}, u32[]{:S(2)}) copy-start(s32[2,16]{1,0:T(2,128)} %param.12) | copy-start | bytes 388
  23.2 16.1 %all-to-all-start.1 = ((bf16[8,16,2,512]{3,2,0,1:T(2,128)(2,1)}), bf16[8,16,2,512]{3,2,0,1:T(2,128)(2,1)S(1)}, u32[]{:S(2)}, u32[]{:S(2)}) async-start(bf16[8,16,2,512]{3,2,0,1:T(2,128)(2,1)} %fusion.32), calls=%async_computation.1 | async-start | bytes 524288 | tf_op jit(solution)/shard_map/all_to_all | solution.py:75
  29.3 0.9 %copy-start.1 = (bf16[4,16,2,512]{3,1,0,2:T(8,128)(2,1)}, bf16[4,16,2,512]{3,1,0,2:T(8,128)(2,1)S(1)}, u32[]{:S(2)}) copy-start(bf16[4,16,2,512]{3,1,0,2:T(8,128)(2,1)S(1)} %copy.18) | copy-start | bytes 393220
  40.8 0.9 %copy-start.2 = (bf16[4,16,2,512]{3,1,0,2:T(8,128)(2,1)S(1)}, bf16[4,16,2,512]{3,1,0,2:T(8,128)(2,1)}, u32[]{:S(2)}) copy-start(bf16[4,16,2,512]{3,1,0,2:T(8,128)(2,1)} %copy-done.1) | copy-start | bytes 393220
where the time goes:
time: 48.2 us; the launch traced here: 47.7 us
  starting transfers between devices  13.4 us (28%)
  matrix products  9.77 us (20%)
  waiting for transfers between devices  8.72 us (18%)
  other arithmetic  7.01 us (15%)
  local copies, waits for them, and re-layouts  6.53 us (14%)
  between operations  2.33 us (5%)
    all_to_all x1, waiting for transfers between devices, body(): lax.all_to_all(outgoing, 'ctx', split_axis=1, concat_axis=1, tiled=True)  8.72 us
    all_to_all x1, starting transfers between devices, body(): lax.all_to_all(prompt_copies, 'ctx', split_axis=1, concat_axis=1, tiled=T...  7.36 us
    all_to_all x1, starting transfers between devices, body(): lax.all_to_all(outgoing, 'ctx', split_axis=1, concat_axis=1, tiled=True)  6 us
    dot_general x12, matrix products, level_part(): jnp.einsum('qd,kd->qk', queries, key_rows, preferred_element_type=jnp.flo...  5.17 us
    dot_general x12, matrix products, level_part(): weighted = jnp.dot(weights, value_rows, preferred_element_type=jnp.float32)  4.61 us
    convert_element_type x6, other arithmetic, level_part(): weights = lax.optimization_barrier(weights.astype(jnp.bfloat16))  2.32 us
    select_n x2, other arithmetic, body(): outgoing = jnp.take(parent_kv, fork_list, axis=1)  1.68 us
    slice x1, local copies, waits for them, and re-layouts, head_rows(): queries[:, kv_head * group_size * head_dim:(kv_head + 1) * group_size * h...  1.31 us
  transfers between devices with their start and end apart: 2, of which 1 were waited for; matrix products, arithmetic and copies ran while one was open for 29% of the time, Pallas kernels for 0%

commit v1 on v0

--- a/solution.py
+++ b/solution.py
@@ -1,10 +1,21 @@
+import functools
+import math
+
 import jax
 import jax.numpy as jnp
 from jax import lax
+from jax.experimental import pallas as pl
+from jax.experimental.pallas import tpu as pltpu
 from jax.sharding import PartitionSpec as P
 
 KVH = 4
 HD = 128
+MESH = pl.DeviceIdType.MESH
+CORES = 2
+COLS = 2
+NEG = -1e30
+HEADS_PER_BLOCK = 4
+GATHER_LIMIT = 4 * 1024 * 1024
 
 
 def head_rows(queries, kv_head, group_size, head_dim):
@@ -102,6 +113,253 @@
     return jnp.concatenate(results, axis=1).astype(jnp.bfloat16)[None]
 
 
+def cascade_kernel(
+    axis_size,
+    q_hbm,
+    kv_hbm,
+    prompt_hbm,
+    parent_hbm,
+    fork_hbm,
+    owner_hbm,
+    length_hbm,
+    out_hbm,
+    q_ref,
+    kv_ref,
+    pool,
+    acc_ref,
+    top_ref,
+    out_ref,
+    fork_ref,
+    owner_ref,
+    length_ref,
+    local_sem,
+    send_sem,
+    recv_sem,
+    out_sem,
+):
+    me = lax.axis_index("ctx")
+    rows_z = axis_size // (CORES * COLS)
+    core = lax.rem(me, CORES)
+    col = lax.rem(me // CORES, COLS)
+    z = me // (CORES * COLS)
+    sibling = me + 1 - 2 * core
+    across = me + CORES - 2 * CORES * col
+    stride = CORES * COLS
+
+    def place(zz, xx, cc):
+        return (zz * COLS + xx) * CORES + cc
+
+    z_peers = [place(lax.rem(z + d, rows_z), col, core) for d in range(1, rows_z)]
+    peers = z_peers + [across, sibling]
+
+    barrier = pltpu.get_barrier_semaphore()
+    for peer in peers:
+        pl.semaphore_signal(barrier, inc=1, device_id={"ctx": peer}, device_id_type=MESH)
+
+    prompt_rows = prompt_hbm.shape[0]
+    seg_rows, parents = parent_hbm.shape[:2]
+    staging = [pltpu.make_async_copy(prompt_hbm, pool.at[me, pl.ds(0, prompt_rows)], local_sem.at[0])]
+    for p in range(parents):
+        staging.append(
+            pltpu.make_async_copy(
+                parent_hbm.at[:, p],
+                pool.at[me, pl.ds(prompt_rows + p * seg_rows, seg_rows)],
+                local_sem.at[1 + p],
+            )
+        )
+    loads = [
+        pltpu.make_async_copy(src, dst, local_sem.at[1 + parents + i])
+        for i, (src, dst) in enumerate(
+            [
+                (kv_hbm.at[0], kv_ref),
+                (q_hbm.at[0], q_ref),
+                (fork_hbm, fork_ref),
+                (owner_hbm, owner_ref),
+                (length_hbm, length_ref),
+            ]
+        )
+    ]
+    for copy in staging + loads:
+        copy.start()
+    for copy in staging:
+        copy.wait()
+    pl.semaphore_wait(barrier, len(peers))
+
+    sends = []
+
+    def send(slot, target):
+        copy = pltpu.make_async_remote_copy(
+            src_ref=pool.at[slot],
+            dst_ref=pool.at[slot],
+            send_sem=send_sem.at[len(sends)],
+            recv_sem=recv_sem.at[slot],
+            device_id={"ctx": target},
+            device_id_type=MESH,
+        )
+        copy.start()
+        sends.append(copy)
+
+    def arrive(slot):
+        pltpu.make_async_remote_copy(
+            src_ref=pool.at[slot],
+            dst_ref=pool.at[slot],
+            send_sem=send_sem.at[0],
+            recv_sem=recv_sem.at[slot],
+            device_id={"ctx": sibling},
+            device_id_type=MESH,
+        ).wait_recv()
+
+    for peer in [across] + z_peers + [sibling]:
+        send(me, peer)
+
+    span, width = q_ref.shape
+    kv_width = kv_ref.shape[2]
+    group = width // kv_width
+    rate = math.log2(math.e) / math.sqrt(HD)
+    block = min(HEADS_PER_BLOCK, group)
+    block_rows = block * span
+
+    def block_queries(first):
+        return jnp.concatenate(
+            [q_ref[:, (first + i) * HD : (first + i + 1) * HD] for i in range(block)], axis=0
+        )
+
+    def scored(queries, keys):
+        return lax.dot_general(
+            queries, keys, (((1,), (1,)), ((), ())), preferred_element_type=jnp.float32
+        )
+
+    def with_ones(values):
+        return jnp.concatenate([values, jnp.ones_like(values)], axis=1)
+
+    for copy in loads[:2]:
+        copy.wait()
+    row_time = lax.rem(lax.broadcasted_iota(jnp.int32, (block_rows, span), 0), span)
+    causal = lax.broadcasted_iota(jnp.int32, (block_rows, span), 1) <= row_time
+
+    def own_level(kv_head):
+        low = kv_head * HD
+        keys = kv_ref[:, 0, low : low + HD]
+        values = with_ones(kv_ref[:, 1, low : low + HD])
+        for first in range(kv_head * group, (kv_head + 1) * group, block):
+            rows = slice(first * span, first * span + block_rows)
+            scores = jnp.where(causal, scored(block_queries(first), keys), NEG)
+            highest = jnp.max(scores, axis=1, keepdims=True)
+            weights = jnp.exp2((scores - highest) * rate).astype(jnp.bfloat16)
+            acc_ref[rows, :] = jnp.dot(weights, values, preferred_element_type=jnp.float32)
+            top_ref[rows, :] = jnp.broadcast_to(highest, (block_rows, HD))
+
+    kv_heads = kv_width // HD
+    half = kv_heads // 2
+    for kv_head in range(half):
+        own_level(kv_head)
+    for d, peer in enumerate(z_peers):
+        arrive(peer)
+        send(peer, across)
+        send(peer, sibling)
+    for kv_head in range(half, kv_heads):
+        own_level(kv_head)
+    far = [place(lax.rem(z + d, rows_z), 1 - col, core) for d in range(rows_z)]
+    for slot in far:
+        arrive(slot)
+        send(slot, sibling)
+
+    for copy in loads[2:]:
+        copy.wait()
+    parent = fork_ref[me]
+    live = length_ref[parent]
+    stored = axis_size * seg_rows
+    lane = lax.broadcasted_iota(jnp.int32, (1, stored), 1)
+    owner_lane, within = lane // seg_rows, lax.rem(lane, seg_rows)
+    position = jnp.zeros((1, stored), jnp.int32)
+    for j in range(axis_size):
+        position = jnp.where(owner_lane == owner_ref[parent, j], j * seg_rows + within, position)
+    prompt_all = axis_size * prompt_rows
+    bias = jnp.concatenate(
+        [jnp.where(position < live, 0.0, NEG), jnp.zeros((1, prompt_all), jnp.float32)], axis=1
+    )
+
+    for d in range(rows_z):
+        for xx in (col, 1 - col):
+            arrive(place(lax.rem(z + d, rows_z), xx, 1 - core))
+
+    start = prompt_rows + parent * seg_rows
+
+    def gathered(index, low):
+        segment = pool[:, pl.ds(start, seg_rows), index, low : low + HD].reshape(stored, HD)
+        prompt = pool[:, :prompt_rows, index, low : low + HD].reshape(prompt_all, HD)
+        return jnp.concatenate([segment, prompt], axis=0)
+
+    writes = []
+    for kv_head in range(kv_heads):
+        low = kv_head * HD
+        keys = gathered(0, low)
+        values = with_ones(gathered(1, low))
+        for first in range(kv_head * group, (kv_head + 1) * group, block):
+            rows = slice(first * span, first * span + block_rows)
+            scores = scored(block_queries(first), keys) + bias
+            own_top = top_ref[rows, :]
+            highest = jnp.maximum(jnp.max(scores, axis=1, keepdims=True), own_top[:, :1])
+            weights = jnp.exp2((scores - highest) * rate).astype(jnp.bfloat16)
+            part = jnp.dot(weights, values, preferred_element_type=jnp.float32)
+            own_weight = jnp.exp2((own_top - highest) * rate)
+            weighted = acc_ref[rows, :HD] * own_weight + part[:, :HD]
+            totals = acc_ref[rows, HD:] * own_weight + part[:, HD:]
+            result = (weighted / totals).astype(jnp.bfloat16)
+            for i in range(block):
+                out_ref[:, (first + i) * HD : (first + i + 1) * HD] = result[i * span : (i + 1) * span]
+        cols = pl.ds(kv_head * group * HD, group * HD)
+        write = pltpu.make_async_copy(out_ref.at[:, cols], out_hbm.at[0, :, cols], out_sem.at[kv_head])
+        write.start()
+        writes.append(write)
+    for copy in sends:
+        copy.wait_send()
+    for write in writes:
+        write.wait()
+
+
+def cascade(child_q, child_kv, prompt_kv, parent_kv, fork_list, owner_map, lengths):
+    axis_size = lax.axis_size("ctx")
+    span, width = child_q.shape[1:]
+    kv_width = child_kv.shape[3]
+    piece = prompt_kv.shape[0] + parent_kv.shape[0] * parent_kv.shape[1]
+    query_rows = span * (width // HD)
+    anywhere = pl.BlockSpec(memory_space=pl.ANY)
+    return pl.pallas_call(
+        functools.partial(cascade_kernel, axis_size),
+        out_shape=jax.ShapeDtypeStruct(child_q.shape, jnp.bfloat16),
+        in_specs=[anywhere] * 7,
+        out_specs=anywhere,
+        scratch_shapes=[
+            pltpu.VMEM((span, width), jnp.bfloat16),
+            pltpu.VMEM((span, 2, kv_width), jnp.bfloat16),
+            pltpu.VMEM((axis_size, piece, 2, kv_width), jnp.bfloat16),
+            pltpu.VMEM((query_rows, 2 * HD), jnp.float32),
+            pltpu.VMEM((query_rows, HD), jnp.float32),
+            pltpu.VMEM((span, width), jnp.bfloat16),
+            pltpu.SMEM(fork_list.shape, jnp.int32),
+            pltpu.SMEM(owner_map.shape, jnp.int32),
+            pltpu.SMEM(lengths.shape, jnp.int32),
+            pltpu.SemaphoreType.DMA((6 + parent_kv.shape[1],)),
+            pltpu.SemaphoreType.DMA((axis_size - 1,)),
+            pltpu.SemaphoreType.DMA((axis_size,)),
+            pltpu.SemaphoreType.DMA((kv_width // HD,)),
+        ],
+        compiler_params=pltpu.CompilerParams(
+            collective_id=0, has_side_effects=True, vmem_limit_bytes=40 * 1024 * 1024
+        ),
+    )(child_q, child_kv, prompt_kv, parent_kv, fork_list, owner_map, lengths)
+
+
+def choose(child_q, child_kv, prompt_kv, parent_kv, fork_list, owner_map, lengths):
+    axis_size = lax.axis_size("ctx")
+    args = (child_q, child_kv, prompt_kv, parent_kv, fork_list, owner_map, lengths)
+    gathered_bytes = 2 * axis_size * (prompt_kv.size + parent_kv.size)
+    if gathered_bytes <= GATHER_LIMIT and axis_size % (CORES * COLS) == 0:
+        return cascade(*args)
+    return body(*args)
+
+
 def solution(mesh):
     placed = (
         P(("groups", "ctx"), None, None),
@@ -113,7 +371,7 @@
         P("groups"),
     )
     return jax.shard_map(
-        body,
+        choose,
         mesh=mesh,
         in_specs=placed,
         out_specs=P(("groups", "ctx"), None, None),

time: 48.2 us -> 25.9 us (0.54)
  the two profiles are of different devices: /device:TPU:0 before, /device:TPU:1 now
where the time goes in v1:
time: 25.9 us; the launch traced here: 25.6 us
  Pallas kernels  19 us (73%)
  local copies, waits for them, and re-layouts  6.59 us (25%)
    pallas_call x1, Pallas kernels, cascade(): pl.pallas_call(functools.partial(cascade_kernel, axis_size), out_shape=ja...  19 us
    unnamed x15, local copies, waits for them, and re-layouts  6.59 us

profile of v1, /device:TPU:1, one launch (start us, length us, event | category | flops | bytes accessed | tf_op | source)
XLA Modules:
  0.0 25.6 jit_solution(16572665690763083893)
XLA Ops:
  0.0 0.0 copy-start
  0.0 1.2 %copy-done = bf16[1,128,4096]{2,1,0:T(8,128)(2,1)S(1)} copy-done((bf16[1,128,4096]{2,1,0:T(8,128)(2,1)S(1)}, bf16[1,128,4096]{2,1,0:T(8,128)(2,1)}, u32[]{:S(2)}) %copy-start) | copy-done | bytes 1048600
  1.2 0.0 copy-start.1
  1.2 0.9 %copy-done.1 = bf16[1,128,2,512]{3,2,1,0:T(2,128)(2,1)S(1)} copy-done((bf16[1,128,2,512]{3,2,1,0:T(2,128)(2,1)S(1)}, bf16[1,128,2,512]{3,2,1,0:T(2,128)(2,1)}, u32[]{:S(2)}) %copy-start.1) | copy-done | bytes 262168
  2.2 0.0 copy-start.2
  2.2 0.8 %copy-done.2 = bf16[8,2,2,512]{3,2,1,0:T(2,128)(2,1)S(1)} copy-done((bf16[8,2,2,512]{3,2,1,0:T(2,128)(2,1)S(1)}, bf16[8,2,2,512]{3,2,1,0:T(2,128)(2,1)}, u32[]{:S(2)}) %copy-start.2) | copy-done | bytes 32792
  2.9 0.0 copy-start.3
  2.9 0.7 %copy-done.3 = bf16[4,2,512]{2,1,0:T(2,128)(2,1)S(1)} copy-done((bf16[4,2,512]{2,1,0:T(2,128)(2,1)S(1)}, bf16[4,2,512]{2,1,0:T(2,128)(2,1)}, u32[]{:S(2)}) %copy-start.3) | copy-done | bytes 8216
  3.6 0.0 copy-start.4
  3.6 0.7 %copy-done.4 = s32[2,16]{1,0:T(2,128)S(1)} copy-done((s32[2,16]{1,0:T(2,128)S(1)}, s32[2,16]{1,0:T(2,128)}, u32[]{:S(2)}) %copy-start.4) | copy-done | bytes 152
  4.3 0.0 copy-start.5
  4.3 0.7 %copy-done.5 = s32[16]{0:T(128)S(1)} copy-done((s32[16]{0:T(128)S(1)}, s32[16]{0:T(128)}, u32[]{:S(2)}) %copy-start.5) | copy-done | bytes 88
  5.0 0.0 copy-start.6
  5.0 0.7 %copy-done.6 = s32[2]{0:T(128)S(1)} copy-done((s32[2]{0:T(128)S(1)}, s32[2]{0:T(128)}, u32[]{:S(2)}) %copy-start.6) | copy-done | bytes 32
  5.6 19.0 %shard_map.73 = bf16[1,128,4096]{2,1,0:T(8,128)(2,1)S(1)} custom-call(bf16[1,128,4096]{2,1,0:T(8,128)(2,1)S(1)} %copy-done, bf16[1,128,2,512]{3,2,1,0:T(2,128)(2,1)S(1)} %copy-done.1, bf16[4,2,512]{2,1,0:T(2,128)(2,1)S(1)} %copy-done.3, bf16[8,2,2,512]{3,2,1,0:T(2,128)(2,1)S(1)} %copy-done.2, s32[16]{0:T(128)S(1)} %copy-done.5, s32[2,16]{1,0:T(2,128)S(1)} %copy-done.4, ...), custom_call_target="tpu_custom_call" | custom-call | tf_op jit(solution)/shard_map/pallas_call | solution.py:328
  24.6 1.0 %copy.9 = bf16[1,128,4096]{2,1,0:T(8,128)(2,1)} copy(bf16[1,128,4096]{2,1,0:T(8,128)(2,1)S(1)} %shard_map.73) | data formatting | bytes 2097152
Async XLA Ops:
  0.0 1.2 %copy-start = (bf16[1,128,4096]{2,1,0:T(8,128)(2,1)S(1)}, bf16[1,128,4096]{2,1,0:T(8,128)(2,1)}, u32[]{:S(2)}) copy-start(bf16[1,128,4096]{2,1,0:T(8,128)(2,1)} %q_hbm.1) | copy-start | bytes 3145732
  1.2 0.9 %copy-start.1 = (bf16[1,128,2,512]{3,2,1,0:T(2,128)(2,1)S(1)}, bf16[1,128,2,512]{3,2,1,0:T(2,128)(2,1)}, u32[]{:S(2)}) copy-start(bf16[1,128,2,512]{3,2,1,0:T(2,128)(2,1)} %kv_hbm.1) | copy-start | bytes 786436
  2.2 0.8 %copy-start.2 = (bf16[8,2,2,512]{3,2,1,0:T(2,128)(2,1)S(1)}, bf16[8,2,2,512]{3,2,1,0:T(2,128)(2,1)}, u32[]{:S(2)}) copy-start(bf16[8,2,2,512]{3,2,1,0:T(2,128)(2,1)} %parent_hbm.1) | copy-start | bytes 98308
  2.9 0.7 %copy-start.3 = (bf16[4,2,512]{2,1,0:T(2,128)(2,1)S(1)}, bf16[4,2,512]{2,1,0:T(2,128)(2,1)}, u32[]{:S(2)}) copy-start(bf16[4,2,512]{2,1,0:T(2,128)(2,1)} %prompt_hbm.1) | copy-start | bytes 24580
  3.6 0.7 %copy-start.4 = (s32[2,16]{1,0:T(2,128)S(1)}, s32[2,16]{1,0:T(2,128)}, u32[]{:S(2)}) copy-start(s32[2,16]{1,0:T(2,128)} %owner_hbm.1) | copy-start | bytes 388
  4.3 0.7 %copy-start.5 = (s32[16]{0:T(128)S(1)}, s32[16]{0:T(128)}, u32[]{:S(2)}) copy-start(s32[16]{0:T(128)} %fork_hbm.1) | copy-start | bytes 196
  5.0 0.7 %copy-start.6 = (s32[2]{0:T(128)S(1)}, s32[2]{0:T(128)}, u32[]{:S(2)}) copy-start(s32[2]{0:T(128)} %length_hbm.1) | copy-start | bytes 28

commit v2 on v1

--- a/solution.py
+++ b/solution.py
@@ -324,12 +324,12 @@
     kv_width = child_kv.shape[3]
     piece = prompt_kv.shape[0] + parent_kv.shape[0] * parent_kv.shape[1]
     query_rows = span * (width // HD)
-    anywhere = pl.BlockSpec(memory_space=pl.ANY)
+    anywhere = pl.BlockSpec(memory_space=pltpu.HBM)
     return pl.pallas_call(
         functools.partial(cascade_kernel, axis_size),
         out_shape=jax.ShapeDtypeStruct(child_q.shape, jnp.bfloat16),
         in_specs=[anywhere] * 7,
-        out_specs=anywhere,
+        out_specs=pl.BlockSpec(memory_space=pl.ANY),
         scratch_shapes=[
             pltpu.VMEM((span, width), jnp.bfloat16),
             pltpu.VMEM((span, 2, kv_width), jnp.bfloat16),
@@ -346,7 +346,7 @@
             pltpu.SemaphoreType.DMA((kv_width // HD,)),
         ],
         compiler_params=pltpu.CompilerParams(
-            collective_id=0, has_side_effects=True, vmem_limit_bytes=40 * 1024 * 1024
+            collective_id=0, has_side_effects=True, vmem_limit_bytes=56 * 1024 * 1024
         ),
     )(child_q, child_kv, prompt_kv, parent_kv, fork_list, owner_map, lengths)
 

time: 25.9 us -> 23.3 us (0.90)
  local copies, waits for them, and re-layouts: 6.59 us -> 2.29 us
  Pallas kernels: 19 us -> 20.8 us
    unnamed x15 -> x1, local copies, waits for them, and re-layouts: 6.59 us -> 2.29 us
    pallas_call x1, Pallas kernels: 19 us -> 20.8 us  [cascade(): pl.pallas_call(functools.partial(cascade_kernel, axis_size), out_shape=ja...]
where the time goes in v2:
time: 23.3 us; the launch traced here: 23.1 us
  Pallas kernels  20.8 us (89%)
  local copies, waits for them, and re-layouts  2.29 us (10%)
    pallas_call x1, Pallas kernels, cascade(): pl.pallas_call(functools.partial(cascade_kernel, axis_size), out_shape=ja...  20.8 us
    unnamed x1, local copies, waits for them, and re-layouts  2.29 us

profile of v2, /device:TPU:1, one launch (start us, length us, event | category | flops | bytes accessed | tf_op | source)
XLA Modules:
  0.0 23.1 jit_solution(10306822247175452585)
XLA Ops:
  0.0 20.8 %shard_map.73 = bf16[1,128,4096]{2,1,0:T(8,128)(2,1)} custom-call(bf16[1,128,4096]{2,1,0:T(8,128)(2,1)} %q_hbm.1, bf16[1,128,2,512]{3,2,1,0:T(2,128)(2,1)} %kv_hbm.1, bf16[4,2,512]{2,1,0:T(2,128)(2,1)} %prompt_hbm.1, bf16[8,2,2,512]{3,2,1,0:T(2,128)(2,1)} %parent_hbm.1, s32[16]{0:T(128)} %fork_hbm.1, s32[2,16]{1,0:T(2,128)} %owner_hbm.1, s32[2]{0:T(128)} %length_hbm.1), custom_call_target="tpu_custom_call" | custom-call | tf_op jit(solution)/shard_map/pallas_call | solution.py:328
  20.8 2.3 %copy.9 = bf16[1,128,4096]{2,1,0:T(8,128)(2,1)} copy(bf16[1,128,4096]{2,1,0:T(8,128)(2,1)} %shard_map.73) | data formatting | bytes 2097152

commit v3 on v2

--- a/solution.py
+++ b/solution.py
@@ -122,20 +122,19 @@
     fork_hbm,
     owner_hbm,
     length_hbm,
-    out_hbm,
+    out_ref,
     q_ref,
     kv_ref,
-    pool,
+    near,
+    far,
     acc_ref,
     top_ref,
-    out_ref,
     fork_ref,
     owner_ref,
     length_ref,
     local_sem,
     send_sem,
     recv_sem,
-    out_sem,
 ):
     me = lax.axis_index("ctx")
     rows_z = axis_size // (CORES * COLS)
@@ -158,12 +157,12 @@
 
     prompt_rows = prompt_hbm.shape[0]
     seg_rows, parents = parent_hbm.shape[:2]
-    staging = [pltpu.make_async_copy(prompt_hbm, pool.at[me, pl.ds(0, prompt_rows)], local_sem.at[0])]
+    staging = [pltpu.make_async_copy(prompt_hbm, near.at[me // CORES, pl.ds(0, prompt_rows)], local_sem.at[0])]
     for p in range(parents):
         staging.append(
             pltpu.make_async_copy(
                 parent_hbm.at[:, p],
-                pool.at[me, pl.ds(prompt_rows + p * seg_rows, seg_rows)],
+                near.at[me // CORES, pl.ds(prompt_rows + p * seg_rows, seg_rows)],
                 local_sem.at[1 + p],
             )
         )
@@ -187,30 +186,27 @@
 
     sends = []
 
-    def send(slot, target):
-        copy = pltpu.make_async_remote_copy(
-            src_ref=pool.at[slot],
-            dst_ref=pool.at[slot],
-            send_sem=send_sem.at[len(sends)],
+    def hop(slot, target, into, index):
+        return pltpu.make_async_remote_copy(
+            src_ref=near.at[slot // CORES],
+            dst_ref=into.at[slot // CORES],
+            send_sem=send_sem.at[index],
             recv_sem=recv_sem.at[slot],
             device_id={"ctx": target},
             device_id_type=MESH,
         )
+
+    def send(slot, target, into):
+        copy = hop(slot, target, into, len(sends))
         copy.start()
         sends.append(copy)
 
-    def arrive(slot):
-        pltpu.make_async_remote_copy(
-            src_ref=pool.at[slot],
-            dst_ref=pool.at[slot],
-            send_sem=send_sem.at[0],
-            recv_sem=recv_sem.at[slot],
-            device_id={"ctx": sibling},
-            device_id_type=MESH,
-        ).wait_recv()
-
-    for peer in [across] + z_peers + [sibling]:
-        send(me, peer)
+    def arrive(slot, into):
+        hop(slot, sibling, into, 0).wait_recv()
+
+    for peer in [across] + z_peers:
+        send(me, peer, near)
+    send(me, sibling, far)
 
     span, width = q_ref.shape
     kv_width = kv_ref.shape[2]
@@ -254,71 +250,77 @@
     for kv_head in range(half):
         own_level(kv_head)
     for d, peer in enumerate(z_peers):
-        arrive(peer)
-        send(peer, across)
-        send(peer, sibling)
+        arrive(peer, near)
+        send(peer, across, near)
+        send(peer, sibling, far)
     for kv_head in range(half, kv_heads):
         own_level(kv_head)
-    far = [place(lax.rem(z + d, rows_z), 1 - col, core) for d in range(rows_z)]
-    for slot in far:
-        arrive(slot)
-        send(slot, sibling)
+    across_slots = [place(lax.rem(z + d, rows_z), 1 - col, core) for d in range(rows_z)]
+    for slot in across_slots:
+        arrive(slot, near)
+        send(slot, sibling, far)
 
     for copy in loads[2:]:
         copy.wait()
     parent = fork_ref[me]
     live = length_ref[parent]
-    stored = axis_size * seg_rows
+    pairs = axis_size // CORES
+    stored, prompt_half = pairs * seg_rows, pairs * prompt_rows
     lane = lax.broadcasted_iota(jnp.int32, (1, stored), 1)
-    owner_lane, within = lane // seg_rows, lax.rem(lane, seg_rows)
-    position = jnp.zeros((1, stored), jnp.int32)
-    for j in range(axis_size):
-        position = jnp.where(owner_lane == owner_ref[parent, j], j * seg_rows + within, position)
-    prompt_all = axis_size * prompt_rows
-    bias = jnp.concatenate(
-        [jnp.where(position < live, 0.0, NEG), jnp.zeros((1, prompt_all), jnp.float32)], axis=1
-    )
-
+    owner_lane, within = (lane // seg_rows) * CORES, lax.rem(lane, seg_rows)
+    start = prompt_rows + parent * seg_rows
+
+    def bias_of(side):
+        position = jnp.zeros((1, stored), jnp.int32)
+        for j in range(axis_size):
+            owned = owner_lane + side == owner_ref[parent, j]
+            position = jnp.where(owned, j * seg_rows + within, position)
+        return jnp.concatenate(
+            [jnp.where(position < live, 0.0, NEG), jnp.zeros((1, prompt_half), jnp.float32)], axis=1
+        )
+
+    def gathered(pool, index, low):
+        segment = pool[:, pl.ds(start, seg_rows), index, low : low + HD].reshape(stored, HD)
+        prompt = pool[:, :prompt_rows, index, low : low + HD].reshape(prompt_half, HD)
+        return jnp.concatenate([segment, prompt], axis=0)
+
+    def gathered_level(pool, bias, last):
+        for kv_head in range(kv_heads):
+            low = kv_head * HD
+            keys = gathered(pool, 0, low)
+            values = with_ones(gathered(pool, 1, low))
+            for first in range(kv_head * group, (kv_head + 1) * group, block):
+                rows = slice(first * span, first * span + block_rows)
+                scores = scored(block_queries(first), keys) + bias
+                former_top = top_ref[rows, :]
+                highest = jnp.maximum(jnp.max(scores, axis=1, keepdims=True), former_top)
+                weights = jnp.exp2((scores - highest[:, : scores.shape[1]]) * rate).astype(jnp.bfloat16)
+                part = jnp.dot(weights, values, preferred_element_type=jnp.float32)
+                former = jnp.exp2((former_top - highest) * rate)
+                weighted = acc_ref[rows, :HD] * former + part[:, :HD]
+                totals = acc_ref[rows, HD:] * former + part[:, HD:]
+                if not last:
+                    acc_ref[rows, :HD] = weighted
+                    acc_ref[rows, HD:] = totals
+                    top_ref[rows, :] = highest
+                    continue
+                result = (weighted / totals).astype(jnp.bfloat16)
+                for i in range(block):
+                    cols = slice((first + i) * HD, (first + i + 1) * HD)
+                    out_ref[0, :, cols] = result[i * span : (i + 1) * span]
+
+    near_bias, far_bias = bias_of(core), bias_of(1 - core)
+    gathered_level(near, near_bias, False)
     for d in range(rows_z):
         for xx in (col, 1 - col):
-            arrive(place(lax.rem(z + d, rows_z), xx, 1 - core))
-
-    start = prompt_rows + parent * seg_rows
-
-    def gathered(index, low):
-        segment = pool[:, pl.ds(start, seg_rows), index, low : low + HD].reshape(stored, HD)
-        prompt = pool[:, :prompt_rows, index, low : low + HD].reshape(prompt_all, HD)
-        return jnp.concatenate([segment, prompt], axis=0)
-
-    writes = []
-    for kv_head in range(kv_heads):
-        low = kv_head * HD
-        keys = gathered(0, low)
-        values = with_ones(gathered(1, low))
-        for first in range(kv_head * group, (kv_head + 1) * group, block):
-            rows = slice(first * span, first * span + block_rows)
-            scores = scored(block_queries(first), keys) + bias
-            own_top = top_ref[rows, :]
-            highest = jnp.maximum(jnp.max(scores, axis=1, keepdims=True), own_top[:, :1])
-            weights = jnp.exp2((scores - highest) * rate).astype(jnp.bfloat16)
-            part = jnp.dot(weights, values, preferred_element_type=jnp.float32)
-            own_weight = jnp.exp2((own_top - highest) * rate)
-            weighted = acc_ref[rows, :HD] * own_weight + part[:, :HD]
-            totals = acc_ref[rows, HD:] * own_weight + part[:, HD:]
-            result = (weighted / totals).astype(jnp.bfloat16)
-            for i in range(block):
-                out_ref[:, (first + i) * HD : (first + i + 1) * HD] = result[i * span : (i + 1) * span]
-        cols = pl.ds(kv_head * group * HD, group * HD)
-        write = pltpu.make_async_copy(out_ref.at[:, cols], out_hbm.at[0, :, cols], out_sem.at[kv_head])
-        write.start()
-        writes.append(write)
+            arrive(place(lax.rem(z + d, rows_z), xx, 1 - core), far)
+    gathered_level(far, far_bias, True)
     for copy in sends:
         copy.wait_send()
-    for write in writes:
-        write.wait()
 
 
 def cascade(child_q, child_kv, prompt_kv, parent_kv, fork_list, owner_map, lengths):
+    operands = (child_q, child_kv, prompt_kv, parent_kv, fork_list, owner_map, lengths)
     axis_size = lax.axis_size("ctx")
     span, width = child_q.shape[1:]
     kv_width = child_kv.shape[3]
@@ -329,33 +331,33 @@
         functools.partial(cascade_kernel, axis_size),
         out_shape=jax.ShapeDtypeStruct(child_q.shape, jnp.bfloat16),
         in_specs=[anywhere] * 7,
-        out_specs=pl.BlockSpec(memory_space=pl.ANY),
+        out_specs=pl.BlockSpec(memory_space=pltpu.VMEM),
         scratch_shapes=[
             pltpu.VMEM((span, width), jnp.bfloat16),
             pltpu.VMEM((span, 2, kv_width), jnp.bfloat16),
-            pltpu.VMEM((axis_size, piece, 2, kv_width), jnp.bfloat16),
+            pltpu.VMEM((axis_size // CORES, piece, 2, kv_width), jnp.bfloat16),
+            pltpu.VMEM((axis_size // CORES, piece, 2, kv_width), jnp.bfloat16),
             pltpu.VMEM((query_rows, 2 * HD), jnp.float32),
             pltpu.VMEM((query_rows, HD), jnp.float32),
-            pltpu.VMEM((span, width), jnp.bfloat16),
             pltpu.SMEM(fork_list.shape, jnp.int32),
             pltpu.SMEM(owner_map.shape, jnp.int32),
             pltpu.SMEM(lengths.shape, jnp.int32),
             pltpu.SemaphoreType.DMA((6 + parent_kv.shape[1],)),
             pltpu.SemaphoreType.DMA((axis_size - 1,)),
             pltpu.SemaphoreType.DMA((axis_size,)),
-            pltpu.SemaphoreType.DMA((kv_width // HD,)),
         ],
         compiler_params=pltpu.CompilerParams(
-            collective_id=0, has_side_effects=True, vmem_limit_bytes=56 * 1024 * 1024
+            collective_id=0, has_side_effects=True, vmem_limit_bytes=40 * 1024 * 1024
         ),
-    )(child_q, child_kv, prompt_kv, parent_kv, fork_list, owner_map, lengths)
+    )(*[pltpu.with_memory_space_constraint(operand, pltpu.HBM) for operand in operands])
 
 
 def choose(child_q, child_kv, prompt_kv, parent_kv, fork_list, owner_map, lengths):
     axis_size = lax.axis_size("ctx")
     args = (child_q, child_kv, prompt_kv, parent_kv, fork_list, owner_map, lengths)
     gathered_bytes = 2 * axis_size * (prompt_kv.size + parent_kv.size)
-    if gathered_bytes <= GATHER_LIMIT and axis_size % (CORES * COLS) == 0:
+    half_keys = axis_size // CORES * (prompt_kv.shape[0] + parent_kv.shape[0])
+    if gathered_bytes <= GATHER_LIMIT and axis_size % (CORES * COLS) == 0 and half_keys <= HD:
         return cascade(*args)
     return body(*args)
 

time: 23.3 us -> 18.6 us (0.80)
  the two profiles are of different devices: /device:TPU:1 before, /device:TPU:0 now
where the time goes in v3:
time: 18.6 us; the launch traced here: 18.4 us
  Pallas kernels  17.4 us (94%)
  local copies, waits for them, and re-layouts  0.97 us (5%)
    pallas_call x1, Pallas kernels, cascade(): pl.pallas_call(functools.partial(cascade_kernel, axis_size), out_shape=ja...  17.4 us
    unnamed x1, local copies, waits for them, and re-layouts  0.97 us

profile of v3, /device:TPU:0, one launch (start us, length us, event | category | flops | bytes accessed | tf_op | source)
XLA Modules:
  0.0 18.4 jit_solution(220574077883297923)
XLA Ops:
  0.0 17.4 %shard_map.73 = bf16[1,128,4096]{2,1,0:T(8,128)(2,1)S(1)} custom-call(bf16[1,128,4096]{2,1,0:T(8,128)(2,1)} %q_hbm.1, bf16[1,128,2,512]{3,2,1,0:T(2,128)(2,1)} %kv_hbm.1, bf16[4,2,512]{2,1,0:T(2,128)(2,1)} %prompt_hbm.1, bf16[8,2,2,512]{3,2,1,0:T(2,128)(2,1)} %parent_hbm.1, s32[16]{0:T(128)} %fork_hbm.1, s32[2,16]{1,0:T(2,128)} %owner_hbm.1, s32[2]{0:T(128)} %length_hbm.1), custom_call_target="tpu_custom_call" | custom-call | tf_op jit(solution)/shard_map/pallas_call | solution.py:330
  17.4 1.0 %copy.9 = bf16[1,128,4096]{2,1,0:T(8,128)(2,1)} copy(bf16[1,128,4096]{2,1,0:T(8,128)(2,1)S(1)} %shard_map.73) | data formatting | bytes 2097152
